TPU v7x, 512 devices: a whole 4x8x8 slice. The times are simulated.
512 devices in a mesh: row: 16 (over y, core), col: 32 (over x, z).
Axes of the slice: x: 4, y: 8, z: 8, core: 2. Of those that a mesh axis runs over, the one named last changes fastest.
Arguments:
- tokens: bfloat16 [256, 12288], P('col', 'row'), may hold values from -6 to 6
- w_in: bfloat16 [12288, 24576], P('row', 'col'), may hold values from -0.0546875 to 0.0546875
- w_out: bfloat16 [24576, 12288], P('col', 'row'), may hold values from -0.0390625 to 0.0390625
- grad_out: bfloat16 [256, 12288], P('col', 'row'), may hold values from -6 to 6
Outputs:
- output: bfloat16 [256, 12288], P('col', 'row')
- grad_tokens: bfloat16 [256, 12288], P('col', 'row')
- grad_w_in: bfloat16 [12288, 24576], P('row', 'col')
- grad_w_out: bfloat16 [24576, 12288], P('col', 'row')
All inputs are finite; a program needn't handle non-finite values.
Results may differ from a plain program's by a relative error of at most 0.005.
Values may be sent and summed in bfloat16 or wider, within the bound.
A program may use at most 64 MiB of HBM per device.

v0:
```python
import math

import jax
import jax.numpy as jnp
from jax import lax
from jax.sharding import PartitionSpec as P

gelu_scale = math.sqrt(2.0 / math.pi)


def gelu_parts(hidden):
    inner = gelu_scale * (hidden + 0.044715 * hidden * hidden * hidden)
    tanh_value = jnp.tanh(inner)
    act_value = 0.5 * hidden * (1.0 + tanh_value)
    act_slope = 0.5 * (1.0 + tanh_value) + 0.5 * hidden * (
        1.0 - tanh_value * tanh_value
    ) * gelu_scale * (1.0 + 3.0 * 0.044715 * hidden * hidden)
    return (act_value, act_slope)


def plain_product(left, right):
    return jnp.dot(left, right, preferred_element_type=jnp.float32)


def transposed_product(left, right):
    return lax.dot_general(
        left, right, (((1,), (1,)), ((), ())), preferred_element_type=jnp.float32
    )


def token_product(left, right):
    return lax.dot_general(
        left, right, (((0,), (0,)), ((), ())), preferred_element_type=jnp.float32
    )


def rows_plain(left, right):
    return plain_product(left, right)


def rows_transposed(left, right):
    return transposed_product(left, right)


def local(tokens, w_in, w_out, grad_out):
    tok_full, grad_full = (
        lax.all_gather(tokens, "col", axis=0, tiled=True),
        lax.all_gather(grad_out, "col", axis=0, tiled=True),
    )
    hidden = lax.psum_scatter(rows_plain(tok_full, w_in), "row", scatter_dimension=0, tiled=True)
    act_value, act_slope = gelu_parts(hidden)
    act_full = lax.all_gather(act_value.astype(jnp.bfloat16), "row", axis=0, tiled=True)
    output = lax.psum_scatter(
        rows_plain(act_full, w_out), "col", scatter_dimension=0, tiled=True
    ).astype(jnp.bfloat16)
    grad_w_out = token_product(act_full, grad_full).astype(jnp.bfloat16)
    grad_act = lax.psum_scatter(
        rows_transposed(grad_full, w_out), "row", scatter_dimension=0, tiled=True
    )
    grad_local = (grad_act * act_slope).astype(jnp.bfloat16)
    grad_hidden = lax.all_gather(grad_local, "row", axis=0, tiled=True)
    grad_w_in = token_product(tok_full, grad_hidden).astype(jnp.bfloat16)
    grad_tokens = lax.psum_scatter(
        rows_transposed(grad_hidden, w_in), "col", scatter_dimension=0, tiled=True
    ).astype(jnp.bfloat16)
    return (output, grad_tokens, grad_w_in, grad_w_out)


def solution(mesh):
    in_specs = (P("col", "row"), P("row", "col"), P("col", "row"), P("col", "row"))
    out_specs = (P("col", "row"), P("col", "row"), P("row", "col"), P("col", "row"))
    return jax.shard_map(local, mesh=mesh, in_specs=in_specs, out_specs=out_specs, check_vma=False)
```

profile of v0, /device:TPU:1, one launch (start us, length us, event | category | flops | bytes accessed | tf_op | source)
XLA Modules:
  0.0 646.5 jit_solution(1369991445207593572)
XLA Ops:
  7.2 0.0 copy-start
  7.2 0.0 reduce-scatter.9.cloned.1.call-start
  7.2 44.5 %all_gather.14 = bf16[256,768]{1,0:T(8,128)(2,1)S(1)} all-gather(bf16[8,768]{1,0:T(8,128)(2,1)} %param.7), channel_id=1, replica_groups=mesh['row'=16,'col'=32] {'col'}, dimensions={0}, use_global_device_ids=true | all-gather | bytes 405504 | tf_op jit(solution)/shard_map/all_gather | solution.py:48
  51.7 0.0 copy-done
  51.7 0.0 copy-start.3
  51.7 1.4 fusion.10
  53.1 0.0 reduce-scatter.9.cloned.1.call-update
  53.2 0.0 reduce-scatter.5.cloned.1.call-start
  53.2 0.0 copy-done.3
  53.2 36.2 %all_gather.12 = bf16[256,768]{1,0:T(8,128)(2,1)S(1)} all-gather(bf16[8,768]{1,0:T(8,128)(2,1)S(1)} %copy-done.3), channel_id=1, replica_groups=mesh['row'=16,'col'=32] {'col'}, dimensions={0}, use_global_device_ids=true | all-gather | bytes 405504 | tf_op jit(solution)/shard_map/all_gather | solution.py:47
  89.4 0.0 copy-done.1
  89.4 1.4 fusion.8
  90.8 0.0 reduce-scatter.5.cloned.1.call-update
  90.8 0.0 reduce-scatter.7.cloned.1.call-start
  90.8 29.1 %reduce-scatter.9.cloned.1.call-done = f32[16,768]{1,0:T(8,128)} async-done(((f32[256,768]{1,0:T(8,128)}), f32[16,768]{1,0:T(8,128)}) %reduce-scatter.9.cloned.1.call-update) | async-done | bytes 49168 | tf_op jit(solution)/shard_map/reduce_scatter | solution.py:57
  120.0 61.7 %reduce-scatter.5.cloned.1.call-done = f32[16,768]{1,0:T(8,128)} async-done(((f32[256,768]{1,0:T(8,128)}), f32[16,768]{1,0:T(8,128)}) %reduce-scatter.5.cloned.1.call-update) | async-done | bytes 49168 | tf_op jit(solution)/shard_map/reduce_scatter | solution.py:50
  181.7 1.5 fusion.7
  183.2 17.5 %all_gather.13 = bf16[256,768]{1,0:T(8,128)(2,1)S(1)} all-gather(bf16[16,768]{1,0:T(8,128)(2,1)S(1)} %get-tuple-element.9), channel_id=1, replica_groups=mesh['row'=16,'col'=32] {'row'}, dimensions={0}, use_global_device_ids=true | all-gather | bytes 417792 | tf_op jit(solution)/shard_map/all_gather | solution.py:52
  200.7 1.4 fusion.9
  202.1 0.0 reduce-scatter.7.cloned.1.call-update
  202.1 0.0 reduce-scatter.11.cloned.1.call-start
  202.1 17.4 %all_gather.15 = bf16[256,768]{1,0:T(8,128)(2,1)S(1)} all-gather(bf16[16,768]{1,0:T(8,128)(2,1)} %get-tuple-element.8), channel_id=1, replica_groups=mesh['row'=16,'col'=32] {'row'}, dimensions={0}, use_global_device_ids=true | all-gather | bytes 417792 | tf_op jit(solution)/shard_map/all_gather | solution.py:61
  219.5 0.7 copy-done.2
  220.3 1.4 fusion.11
  221.7 0.0 reduce-scatter.11.cloned.1.call-update
  221.7 1.5 fusion
  223.2 1.5 copy.8
  224.7 1.5 convolution_convert_fusion
  226.2 190.1 %reduce-scatter.7.cloned.1.call-done = f32[8,768]{1,0:T(8,128)} async-done(((f32[256,768]{1,0:T(8,128)}), f32[8,768]{1,0:T(8,128)}) %reduce-scatter.7.cloned.1.call-update) | async-done | bytes 24592 | tf_op jit(solution)/shard_map/reduce_scatter | solution.py:53
  416.3 1.3 convert_element_type.22
  417.6 221.0 %reduce-scatter.11.cloned.1.call-done = f32[8,768]{1,0:T(8,128)} async-done(((f32[256,768]{1,0:T(8,128)}), f32[8,768]{1,0:T(8,128)}) %reduce-scatter.11.cloned.1.call-update) | async-done | bytes 24592 | tf_op jit(solution)/shard_map/reduce_scatter | solution.py:63
  638.6 1.3 convert_element_type.24
  (2 shorter events, 0.0 us)
Async XLA Ops:
  7.2 44.6 %copy-start = (bf16[768,768]{1,0:T(8,128)(2,1)S(1)}, bf16[768,768]{1,0:T(8,128)(2,1)}, u32[]{:S(2)}) copy-start(bf16[768,768]{1,0:T(8,128)(2,1)} %param.6) | copy-start | bytes 3538948
  7.2 112.8 %reduce-scatter.9.cloned.1.call-start = ((), (), s32[]{:S(2)}) async-start(), calls=%async_computation.6 | async-start | bytes 835584 | tf_op jit(solution)/shard_map/reduce_scatter | solution.py:57
  51.7 1.5 copy-start.3
  53.1 36.3 %copy-start.1 = (bf16[768,768]{1,0:T(8,128)(2,1)S(1)}, bf16[768,768]{1,0:T(8,128)(2,1)}, u32[]{:S(2)}) copy-start(bf16[768,768]{1,0:T(8,128)(2,1)} %param.5) | copy-start | bytes 3538948
  53.2 128.6 %reduce-scatter.5.cloned.1.call-start = ((), (), s32[]{:S(2)}) async-start(), calls=%async_computation.4 | async-start | bytes 835584 | tf_op jit(solution)/shard_map/reduce_scatter | solution.py:50
  90.8 325.5 %reduce-scatter.7.cloned.1.call-start = ((), (), s32[]{:S(2)}) async-start(), calls=%async_computation.5 | async-start | bytes 811008 | tf_op jit(solution)/shard_map/reduce_scatter | solution.py:53
  202.1 436.5 %reduce-scatter.11.cloned.1.call-start = ((), (), s32[]{:S(2)}) async-start(), calls=%async_computation.7 | async-start | bytes 811008 | tf_op jit(solution)/shard_map/reduce_scatter | solution.py:63
  219.5 0.7 copy-start.2
Sparse Core Ops, SparseCore 0:
  53.3 66.6 reduce-scatter.8
  123.6 58.0 reduce-scatter.4
  202.2 214.0 reduce-scatter.6
  420.5 218.0 reduce-scatter.10
where the time goes:
time: 651 us; the launch traced here: 646 us
  waiting for transfers between devices  502 us (77%)
  blocking collectives  116 us (18%)
  between operations  13.8 us (2%)
  matrix products  8.55 us (1%)
    reduce_scatter x1, waiting for transfers between devices, local(): lax.psum_scatter(rows_transposed(grad_hidden, w_in), 'col', scatter_dimen...  221 us
    reduce_scatter x1, waiting for transfers between devices, local(): lax.psum_scatter(rows_plain(act_full, w_out), 'col', scatter_dimension=0,...  190 us
    reduce_scatter x1, waiting for transfers between devices, local(): lax.psum_scatter(rows_plain(tok_full, w_in), 'row', scatter_dimension=0,...  61.7 us
    all_gather x1, blocking collectives, local(): lax.all_gather(grad_out, 'col', axis=0, tiled=True)  44.5 us
    all_gather x1, blocking collectives, local(): lax.all_gather(tokens, 'col', axis=0, tiled=True)  36.2 us
    reduce_scatter x1, waiting for transfers between devices, local(): lax.psum_scatter(rows_transposed(grad_full, w_out), 'row', scatter_dimens...  29.1 us
    all_gather x1, blocking collectives, local(): lax.all_gather(act_value.astype(jnp.bfloat16), 'row', axis=0, tiled=True)  17.5 us
    all_gather x1, blocking collectives, local(): grad_hidden = lax.all_gather(grad_local, 'row', axis=0, tiled=True)  17.4 us
  transfers between devices with their start and end apart: 4, of which 4 were waited for; matrix products, arithmetic and copies ran while one was open for 1% of the time, Pallas kernels for 0%

commit v1 on v0

v1 whole, which is shorter than its diff:
```python
import functools
import math

import jax
import jax.numpy as jnp
from jax import lax
from jax.experimental import pallas as pl
from jax.experimental.pallas import tpu as pltpu
from jax.sharding import PartitionSpec as P

gelu_scale = math.sqrt(2.0 / math.pi)
MESH = pl.DeviceIdType.MESH
F32 = jnp.float32
BF16 = jnp.bfloat16

NX = 4
OFFSETS = (0, 1, 3, 2)
BACK = (0, 2, 1, 3)
GROUPS = ((0,), (1, 2), (3,))


def gelu_parts(hidden):
    inner = gelu_scale * (hidden + 0.044715 * hidden * hidden * hidden)
    tanh_value = jnp.tanh(inner)
    act_value = 0.5 * hidden * (1.0 + tanh_value)
    act_slope = 0.5 * (1.0 + tanh_value) + 0.5 * hidden * (
        1.0 - tanh_value * tanh_value
    ) * gelu_scale * (1.0 + 3.0 * 0.044715 * hidden * hidden)
    return (act_value, act_slope)


def mm(left, right):
    return jnp.dot(left, right, preferred_element_type=F32)


def far_first(n):
    return sorted(range(1, n), key=lambda k: (-min(k, n - k), k))


def scratch_list(ny, nz, width, hid):
    half, chunk = hid // 2, nz * 8
    s = {
        "win": pltpu.VMEM((width, hid), BF16),
        "wout": pltpu.VMEM((hid, width), BF16),
        "win_t": pltpu.VMEM((hid, width), BF16),
        "wout_t": pltpu.VMEM((width, hid), BF16),
        "act_t": pltpu.VMEM((hid, NX * chunk), BF16),
        "tok_t": pltpu.VMEM((width, NX * chunk), BF16),
        "comb": pltpu.VMEM((nz, 16, width), BF16),
        "tg": pltpu.VMEM((NX, 2, chunk, width), BF16),
        "actb": pltpu.VMEM((NX, chunk, hid), BF16),
        "ghb": pltpu.VMEM((NX, chunk, hid), BF16),
        "ds": pltpu.VMEM((NX, 2, chunk, width), BF16),
        "dr": pltpu.VMEM((NX, 2, chunk, width), BF16),
        "down": pltpu.VMEM((2, chunk, width), F32),
        "zs": pltpu.VMEM((nz, 16, width), BF16),
        "zr": pltpu.VMEM((nz, 16, width), BF16),
    }
    for g, slots in enumerate(GROUPS):
        n = len(slots)
        s[f"hk{g}"] = pltpu.VMEM((2, n * chunk, half), F32)
        s[f"xs{g}"] = pltpu.VMEM((2, n * chunk, half), F32)
        s[f"xr{g}"] = pltpu.VMEM((2, n * chunk, half), F32)
        s[f"bs{g}"] = pltpu.VMEM((ny, n * 16, half), BF16)
        s[f"br{g}"] = pltpu.VMEM((ny, n * 16, half), BF16)
        s[f"cb{g}"] = pltpu.VMEM((2, ny, n * 16, half), BF16)
    dma = pltpu.SemaphoreType.DMA
    ng = len(GROUPS)
    s["w_sem"] = dma((4,))
    for name, shape in (
        ("az", (nz,)),
        ("ax", (NX,)),
        ("cx", (ng,)),
        ("by", (ng, ny)),
        ("cy", (ng, ny)),
        ("cf", (ng,)),
        ("dx", (NX,)),
        ("dz", (nz,)),
    ):
        s[name + "_s"] = dma(shape)
        s[name + "_r"] = dma(shape)
    return s


def kernel(ny, nz, names, tok_ref, grad_ref, win_hbm, wout_hbm, out_ref, gt_ref, gwin_ref, gwout_ref, *scratch):
    r = dict(zip(names, scratch))
    width, hid = r["win"].shape
    half, chunk = hid // 2, nz * 8
    row, col = lax.axis_index("row"), lax.axis_index("col")
    y, core = row // 2, lax.rem(row, 2)
    x, z = col // nz, lax.rem(col, nz)
    sibling = {"row": y * 2 + (1 - core), "col": col}

    def at_y(k):
        return {"row": lax.rem(y + k, ny) * 2 + core, "col": col}

    def at_x(k):
        return {"row": row, "col": lax.rem(x + k, NX) * nz + z}

    def at_z(k):
        return {"row": row, "col": x * nz + lax.rem(z + k, nz)}

    sent = []

    def send(src, dst, sem, send_at, recv_at, device):
        copy = pltpu.make_async_remote_copy(
            src_ref=src,
            dst_ref=dst,
            send_sem=r[sem + "_s"].at[send_at],
            recv_sem=r[sem + "_r"].at[recv_at],
            device_id=device,
            device_id_type=MESH,
        )
        copy.start()
        sent.append(copy)
        return copy

    weight_copies = []
    for h in range(2):
        start = pl.multiple_of((core if h == 0 else 1 - core) * half, half)
        weight_copies.append(
            pltpu.make_async_copy(
                win_hbm.at[:, pl.ds(start, half)], r["win"].at[:, pl.ds(h * half, half)], r["w_sem"].at[h]
            )
        )
        weight_copies.append(
            pltpu.make_async_copy(
                wout_hbm.at[pl.ds(start, half), :], r["wout"].at[pl.ds(h * half, half), :], r["w_sem"].at[2 + h]
            )
        )
    for copy in weight_copies:
        copy.start()

    barrier = pltpu.get_barrier_semaphore()
    partners = (
        [at_z(k) for k in range(1, nz)]
        + [at_x(k) for k in range(1, NX)]
        + [at_y(k) for k in range(1, ny)]
        + [sibling]
    )
    for device in partners:
        pl.semaphore_signal(barrier, inc=1, device_id=device, device_id_type=MESH)
    r["comb"][z] = jnp.concatenate(
        [tok_ref[...].astype(F32), grad_ref[...].astype(F32)], axis=0
    ).astype(BF16)
    pl.semaphore_wait(barrier, len(partners))

    az = [
        send(r["comb"].at[z], r["comb"].at[z], "az", k, nz - k, at_z(k)) for k in far_first(nz)
    ]
    for copy in weight_copies:
        copy.wait()
    r["wout_t"][...] = r["wout"][...].T
    r["win_t"][...] = r["win"][...].T
    for copy in az:
        copy.wait_recv()
    block = r["comb"][...].astype(F32)
    r["tg"][0, 0] = block[:, :8, :].reshape(chunk, width).astype(BF16)
    r["tg"][0, 1] = block[:, 8:, :].reshape(chunk, width).astype(BF16)

    ax = {}
    for s in (1, 2, 3):
        ax[BACK[s]] = send(r["tg"].at[0], r["tg"].at[BACK[s]], "ax", s, BACK[s], at_x(OFFSETS[s]))

    live = {}

    def rows_of(name, part, slots):
        return jnp.concatenate([r[name][s, part] for s in slots], axis=0)

    def first_products(g):
        slots = GROUPS[g]
        for s in slots:
            if s:
                ax[s].wait_recv()
        hidden = mm(rows_of("tg", 0, slots), r["win"][...])
        grad_act = mm(rows_of("tg", 1, slots), r["wout_t"][...])
        for i, value in enumerate((hidden, grad_act)):
            r[f"xs{g}"][i] = value[:, half:]
            r[f"hk{g}"][i] = value[:, :half]
        live["cx", g] = send(r[f"xs{g}"], r[f"xr{g}"], "cx", g, g, sibling)

    def terms_over_y(g):
        n = len(GROUPS[g])
        live["cx", g].wait_recv()
        both = [r[f"hk{g}"][i] + r[f"xr{g}"][i] for i in range(2)]
        for d in range(ny):
            parts = []
            for i in range(n):
                for j in range(2):
                    at = i * chunk + d * 8
                    parts.append(both[j][at : at + 8])
            r[f"bs{g}"][d] = jnp.concatenate(parts, axis=0).astype(BF16)
        live["by", g] = [
            send(r[f"bs{g}"].at[lax.rem(y + k, ny)], r[f"br{g}"].at[ny - k], "by", (g, k), (g, ny - k), at_y(k))
            for k in far_first(ny)
        ]

    def activate(g):
        n = len(GROUPS[g])
        total = r[f"bs{g}"][y].astype(F32)
        for copy in live["by", g]:
            copy.wait_recv()
        for k in range(1, ny):
            total = total + r[f"br{g}"][k].astype(F32)
        total = total.reshape(n, 2, 8, half)
        act_value, act_slope = gelu_parts(total[:, 0])
        grad_hidden = total[:, 1] * act_slope
        both = jnp.stack([act_value, grad_hidden], axis=1).reshape(n * 16, half)
        r[f"cb{g}"][0, y] = both.astype(BF16)
        own = r[f"cb{g}"].at[0, y]
        live["cy", g] = [
            send(own, own, "cy", (g, k), (g, ny - k), at_y(k)) for k in far_first(ny)
        ]

    def forward(g):
        for copy in live["cy", g]:
            copy.wait_recv()
        live["cf", g] = send(r[f"cb{g}"].at[0], r[f"cb{g}"].at[1], "cf", g, g, sibling)

    def second_products(g):
        slots = GROUPS[g]
        n = len(slots)
        live["cf", g].wait_recv()
        for h in range(2):
            got = r[f"cb{g}"][h].astype(F32).reshape(ny, n, 2, 8, half)
            for i, s in enumerate(slots):
                r["actb"][s, :, h * half : (h + 1) * half] = got[:, i, 0].reshape(chunk, half).astype(BF16)
                r["ghb"][s, :, h * half : (h + 1) * half] = got[:, i, 1].reshape(chunk, half).astype(BF16)
        first, last = slots[0], slots[-1] + 1
        act = r["actb"][first:last].reshape(n * chunk, hid)
        grad_hidden = r["ghb"][first:last].reshape(n * chunk, hid)
        for j, value in enumerate((mm(act, r["wout"][...]), mm(grad_hidden, r["win_t"][...]))):
            for i, s in enumerate(slots):
                part = value[i * chunk : (i + 1) * chunk]
                if s:
                    r["ds"][s, j] = part.astype(BF16)
                else:
                    r["down"][j] = part
        for s in slots:
            if s:
                live["dx", BACK[s]] = send(
                    r["ds"].at[s], r["dr"].at[BACK[s]], "dx", s, BACK[s], at_x(OFFSETS[s])
                )

    first_products(0)
    terms_over_y(0)
    activate(0)
    first_products(1)
    forward(0)
    terms_over_y(1)
    second_products(0)
    first_products(2)
    activate(1)
    terms_over_y(2)
    forward(1)
    activate(2)
    second_products(1)
    forward(2)
    second_products(2)

    tile = min(256, half)
    tokens_all = rows_of("tg", 0, range(NX))
    grad_all = rows_of("tg", 1, range(NX))
    r["act_t"][...] = r["actb"][...].reshape(NX * chunk, hid).T
    r["tok_t"][...] = tokens_all.T
    grad_hidden_all = r["ghb"][...].reshape(NX * chunk, hid)
    for h in range(2):
        start = pl.multiple_of((core if h == 0 else 1 - core) * half, half)
        gwout_ref[pl.ds(start, half), :] = mm(
            r["act_t"][h * half : (h + 1) * half, :], grad_all
        ).astype(BF16)
        gwin_ref[:, pl.ds(start, half)] = mm(
            r["tok_t"][...], grad_hidden_all[:, h * half : (h + 1) * half]
        ).astype(BF16)

    for s in (1, 2, 3):
        live["dx", s].wait_recv()
    sums = []
    for j in range(2):
        value = r["down"][j]
        for s in (1, 2, 3):
            value = value + r["dr"][s, j].astype(F32)
        sums.append(value)
    for d in range(nz):
        r["zs"][d] = jnp.concatenate([v[d * 8 : d * 8 + 8] for v in sums], axis=0).astype(BF16)
    dz = [
        send(r["zs"].at[lax.rem(z + k, nz)], r["zr"].at[nz - k], "dz", k, nz - k, at_z(k)) for k in far_first(nz)
    ]
    total = r["zs"][z].astype(F32)
    for copy in dz:
        copy.wait_recv()
    for k in range(1, nz):
        total = total + r["zr"][k].astype(F32)
    out_ref[...] = total[:8].astype(BF16)
    gt_ref[...] = total[8:].astype(BF16)
    for copy in sent:
        copy.wait_send()


def local(ny, nz, tokens, w_in, w_out, grad_out):
    width, hid = w_in.shape
    scratch = scratch_list(ny, nz, width, hid)
    vmem = pl.BlockSpec(memory_space=pltpu.VMEM)
    any_space = pl.BlockSpec(memory_space=pl.ANY)
    return pl.pallas_call(
        functools.partial(kernel, ny, nz, tuple(scratch)),
        out_shape=(
            jax.ShapeDtypeStruct((8, width), BF16),
            jax.ShapeDtypeStruct((8, width), BF16),
            jax.ShapeDtypeStruct((width, hid), BF16),
            jax.ShapeDtypeStruct((hid, width), BF16),
        ),
        in_specs=[vmem, vmem, any_space, any_space],
        out_specs=(vmem, vmem, vmem, vmem),
        scratch_shapes=list(scratch.values()),
        compiler_params=pltpu.CompilerParams(
            collective_id=0, has_side_effects=True, vmem_limit_bytes=48 * 1024 * 1024
        ),
        name="ffn",
    )(tokens, grad_out, w_in, w_out)


def solution(mesh):
    ny, nz = mesh.shape["row"] // 2, mesh.shape["col"] // NX
    in_specs = (P("col", "row"), P("row", "col"), P("col", "row"), P("col", "row"))
    out_specs = (P("col", "row"), P("col", "row"), P("row", "col"), P("col", "row"))
    return jax.shard_map(
        functools.partial(local, ny, nz), mesh=mesh, in_specs=in_specs, out_specs=out_specs, check_vma=False
    )
```

time: 651 us -> 77.5 us (0.12)
  waiting for transfers between devices: 502 us -> 0 us
  blocking collectives: 116 us -> 0 us
  Pallas kernels: 0 us -> 69.4 us
  between operations: 13.8 us -> 0.65 us
  matrix products: 8.55 us -> 0 us
    reduce_scatter x4 -> x0, waiting for transfers between devices: 502 us -> none  [the longest x1 221 us: local(): lax.psum_scatter(rows_transposed(grad_hidden, w_in), 'col', scatter_dimen...]
    all_gather x4 -> x0, blocking collectives: 116 us -> none  [the longest x1 44.5 us: local(): lax.all_gather(grad_out, 'col', axis=0, tiled=True)]
    pallas_call x0 -> x1, Pallas kernels: none -> 69.4 us  [local(): pl.pallas_call(functools.partial(kernel, ny, nz, tuple(scratch)), out_sha...]
    dot_general x6 -> x0, matrix products: 8.55 us -> none  [the longest x2 3.04 us: token_product(): lax.dot_general(left, right, (((0,), (0,)), ((), ())), preferred_element_...]
  transfers between devices with their start and end apart: 4 -> 0, of which waited for: 4 -> 0; matrix products, arithmetic and copies ran while one was open for 1% -> 0% of each run, Pallas kernels for 0% -> 0%
where the time goes in v1:
time: 77.5 us; the launch traced here: 77.2 us
  Pallas kernels  69.4 us (90%)
  local copies, waits for them, and re-layouts  7.17 us (9%)
    pallas_call x1, Pallas kernels, local(): pl.pallas_call(functools.partial(kernel, ny, nz, tuple(scratch)), out_sha...  69.4 us
    unnamed x12, local copies, waits for them, and re-layouts  7.17 us

profile of v1, /device:TPU:1, one launch (start us, length us, event | category | flops | bytes accessed | tf_op | source)
XLA Modules:
  0.0 77.2 jit_solution(14670694004891120419)
XLA Ops:
  0.6 0.0 copy-start
  0.6 1.3 %copy-done = bf16[768,768]{1,0:T(8,128)(2,1)S(1)} copy-done((bf16[768,768]{1,0:T(8,128)(2,1)S(1)}, bf16[768,768]{1,0:T(8,128)(2,1)}, u32[]{:S(2)}) %copy-start) | copy-done | bytes 1179672
  1.9 0.0 copy-start.1
  1.9 1.3 %copy-done.1 = bf16[768,768]{1,0:T(8,128)(2,1)S(1)} copy-done((bf16[768,768]{1,0:T(8,128)(2,1)S(1)}, bf16[768,768]{1,0:T(8,128)(2,1)}, u32[]{:S(2)}) %copy-start.1) | copy-done | bytes 1179672
  3.2 0.0 copy-start.2
  3.2 0.7 copy-done.2
  3.9 0.0 copy-start.3
  3.9 0.7 copy-done.3
  4.6 69.4 %ffn.1 = (bf16[8,768]{1,0:T(8,128)(2,1)S(1)}, bf16[8,768]{1,0:T(8,128)(2,1)S(1)}, bf16[768,768]{1,0:T(8,128)(2,1)S(1)}, bf16[768,768]{1,0:T(8,128)(2,1)S(1)}) custom-call(bf16[8,768]{1,0:T(8,128)(2,1)S(1)} %copy-done.2, bf16[8,768]{1,0:T(8,128)(2,1)S(1)} %copy-done.3, bf16[768,768]{1,0:T(8,128)(2,1)S(1)} %copy-done, bf16[768,768]{1,0:T(8,128)(2,1)S(1)} %copy-done.1), custom_call_target="tpu_custom_call" | custom-call | tf_op jit(solution)/shard_map/ffn/pallas_call | solution.py:305
  74.0 0.6 copy.12
  74.6 0.6 copy.13
  75.2 1.0 %copy.14 = bf16[768,768]{1,0:T(8,128)(2,1)} copy(bf16[768,768]{1,0:T(8,128)(2,1)S(1)} %get-tuple-element.10) | data formatting | bytes 2359296
  76.2 1.0 %copy.15 = bf16[768,768]{1,0:T(8,128)(2,1)} copy(bf16[768,768]{1,0:T(8,128)(2,1)S(1)} %get-tuple-element.11) | data formatting | bytes 2359296
Async XLA Ops:
  0.6 1.3 %copy-start = (bf16[768,768]{1,0:T(8,128)(2,1)S(1)}, bf16[768,768]{1,0:T(8,128)(2,1)}, u32[]{:S(2)}) copy-start(bf16[768,768]{1,0:T(8,128)(2,1)} %win_hbm.1) | copy-start | bytes 3538948
  1.9 1.3 %copy-start.1 = (bf16[768,768]{1,0:T(8,128)(2,1)S(1)}, bf16[768,768]{1,0:T(8,128)(2,1)}, u32[]{:S(2)}) copy-start(bf16[768,768]{1,0:T(8,128)(2,1)} %wout_hbm.1) | copy-start | bytes 3538948
  3.2 0.7 copy-start.2
  3.9 0.7 copy-start.3

commit v2 on v1

--- a/solution.py
+++ b/solution.py
@@ -16,7 +16,7 @@
 NX = 4
 OFFSETS = (0, 1, 3, 2)
 BACK = (0, 2, 1, 3)
-GROUPS = ((0,), (1, 2), (3,))
+GROUPS = ((0,), (1,), (2,), (3,))
 
 
 def gelu_parts(hidden):
@@ -29,8 +29,16 @@
     return (act_value, act_slope)
 
 
+def mm_t(left, right):
+    return lax.dot_general(left, right, (((1,), (1,)), ((), ())), preferred_element_type=F32)
+
+
 def mm(left, right):
     return jnp.dot(left, right, preferred_element_type=F32)
+
+
+def near_first(n):
+    return sorted(range(1, n), key=lambda k: (min(k, n - k), k))
 
 
 def far_first(n):
@@ -42,17 +50,15 @@
     s = {
         "win": pltpu.VMEM((width, hid), BF16),
         "wout": pltpu.VMEM((hid, width), BF16),
-        "win_t": pltpu.VMEM((hid, width), BF16),
-        "wout_t": pltpu.VMEM((width, hid), BF16),
         "act_t": pltpu.VMEM((hid, NX * chunk), BF16),
         "tok_t": pltpu.VMEM((width, NX * chunk), BF16),
-        "comb": pltpu.VMEM((nz, 16, width), BF16),
+        "comb": pltpu.VMEM((NX, nz, 16, width), BF16),
         "tg": pltpu.VMEM((NX, 2, chunk, width), BF16),
         "actb": pltpu.VMEM((NX, chunk, hid), BF16),
         "ghb": pltpu.VMEM((NX, chunk, hid), BF16),
-        "ds": pltpu.VMEM((NX, 2, chunk, width), BF16),
-        "dr": pltpu.VMEM((NX, 2, chunk, width), BF16),
-        "down": pltpu.VMEM((2, chunk, width), F32),
+        "ds": pltpu.VMEM((NX, nz, 16, width), BF16),
+        "dr": pltpu.VMEM((NX, nz, 16, width), BF16),
+        "down": pltpu.VMEM((nz, 16, width), F32),
         "zs": pltpu.VMEM((nz, 16, width), BF16),
         "zr": pltpu.VMEM((nz, 16, width), BF16),
     }
@@ -61,6 +67,7 @@
         s[f"hk{g}"] = pltpu.VMEM((2, n * chunk, half), F32)
         s[f"xs{g}"] = pltpu.VMEM((2, n * chunk, half), F32)
         s[f"xr{g}"] = pltpu.VMEM((2, n * chunk, half), F32)
+        s[f"bf{g}"] = pltpu.VMEM((ny, n * 16, half), F32)
         s[f"bs{g}"] = pltpu.VMEM((ny, n * 16, half), BF16)
         s[f"br{g}"] = pltpu.VMEM((ny, n * 16, half), BF16)
         s[f"cb{g}"] = pltpu.VMEM((2, ny, n * 16, half), BF16)
@@ -69,12 +76,12 @@
     s["w_sem"] = dma((4,))
     for name, shape in (
         ("az", (nz,)),
-        ("ax", (NX,)),
+        ("ax", (NX, nz)),
         ("cx", (ng,)),
         ("by", (ng, ny)),
         ("cy", (ng, ny)),
         ("cf", (ng,)),
-        ("dx", (NX,)),
+        ("dx", (NX, nz)),
         ("dz", (nz,)),
     ):
         s[name + "_s"] = dma(shape)
@@ -140,27 +147,31 @@
     )
     for device in partners:
         pl.semaphore_signal(barrier, inc=1, device_id=device, device_id_type=MESH)
-    r["comb"][z] = jnp.concatenate(
-        [tok_ref[...].astype(F32), grad_ref[...].astype(F32)], axis=0
-    ).astype(BF16)
+    comb = r["comb"]
+    comb[0, z] = jnp.concatenate([tok_ref[...].astype(F32), grad_ref[...].astype(F32)], axis=0).astype(BF16)
     pl.semaphore_wait(barrier, len(partners))
 
-    az = [
-        send(r["comb"].at[z], r["comb"].at[z], "az", k, nz - k, at_z(k)) for k in far_first(nz)
-    ]
+    az = {k: send(comb.at[0, z], comb.at[0, z], "az", k, nz - k, at_z(k)) for k in near_first(nz)}
+    ax = {}
+
+    def block_over_x(k):
+        part = lax.rem(z + k, nz)
+        for s in (3, 1, 2):
+            ax[BACK[s], k] = send(
+                comb.at[0, part], comb.at[BACK[s], part], "ax", (s, k), (BACK[s], k), at_x(OFFSETS[s])
+            )
+
+    block_over_x(0)
     for copy in weight_copies:
         copy.wait()
-    r["wout_t"][...] = r["wout"][...].T
-    r["win_t"][...] = r["win"][...].T
-    for copy in az:
-        copy.wait_recv()
-    block = r["comb"][...].astype(F32)
-    r["tg"][0, 0] = block[:, :8, :].reshape(chunk, width).astype(BF16)
-    r["tg"][0, 1] = block[:, 8:, :].reshape(chunk, width).astype(BF16)
-
-    ax = {}
-    for s in (1, 2, 3):
-        ax[BACK[s]] = send(r["tg"].at[0], r["tg"].at[BACK[s]], "ax", s, BACK[s], at_x(OFFSETS[s]))
+    for k in near_first(nz):
+        az[nz - k].wait_recv()
+        block_over_x(k)
+
+    def split_chunk(s):
+        block = comb[s].astype(F32)
+        r["tg"][s, 0] = block[:, :8, :].reshape(chunk, width).astype(BF16)
+        r["tg"][s, 1] = block[:, 8:, :].reshape(chunk, width).astype(BF16)
 
     live = {}
 
@@ -171,9 +182,11 @@
         slots = GROUPS[g]
         for s in slots:
             if s:
-                ax[s].wait_recv()
+                for k in range(nz):
+                    ax[s, k].wait_recv()
+            split_chunk(s)
         hidden = mm(rows_of("tg", 0, slots), r["win"][...])
-        grad_act = mm(rows_of("tg", 1, slots), r["wout_t"][...])
+        grad_act = mm_t(rows_of("tg", 1, slots), r["wout"][...])
         for i, value in enumerate((hidden, grad_act)):
             r[f"xs{g}"][i] = value[:, half:]
             r[f"hk{g}"][i] = value[:, :half]
@@ -189,7 +202,9 @@
                 for j in range(2):
                     at = i * chunk + d * 8
                     parts.append(both[j][at : at + 8])
-            r[f"bs{g}"][d] = jnp.concatenate(parts, axis=0).astype(BF16)
+            value = jnp.concatenate(parts, axis=0)
+            r[f"bf{g}"][d] = value
+            r[f"bs{g}"][d] = value.astype(BF16)
         live["by", g] = [
             send(r[f"bs{g}"].at[lax.rem(y + k, ny)], r[f"br{g}"].at[ny - k], "by", (g, k), (g, ny - k), at_y(k))
             for k in far_first(ny)
@@ -197,7 +212,7 @@
 
     def activate(g):
         n = len(GROUPS[g])
-        total = r[f"bs{g}"][y].astype(F32)
+        total = r[f"bf{g}"][y]
         for copy in live["by", g]:
             copy.wait_recv()
         for k in range(1, ny):
@@ -208,9 +223,7 @@
         both = jnp.stack([act_value, grad_hidden], axis=1).reshape(n * 16, half)
         r[f"cb{g}"][0, y] = both.astype(BF16)
         own = r[f"cb{g}"].at[0, y]
-        live["cy", g] = [
-            send(own, own, "cy", (g, k), (g, ny - k), at_y(k)) for k in far_first(ny)
-        ]
+        live["cy", g] = [send(own, own, "cy", (g, k), (g, ny - k), at_y(k)) for k in far_first(ny)]
 
     def forward(g):
         for copy in live["cy", g]:
@@ -229,34 +242,44 @@
         first, last = slots[0], slots[-1] + 1
         act = r["actb"][first:last].reshape(n * chunk, hid)
         grad_hidden = r["ghb"][first:last].reshape(n * chunk, hid)
-        for j, value in enumerate((mm(act, r["wout"][...]), mm(grad_hidden, r["win_t"][...]))):
-            for i, s in enumerate(slots):
-                part = value[i * chunk : (i + 1) * chunk]
+        out_part = mm(act, r["wout"][...])
+        grad_part = mm_t(grad_hidden, r["win"][...])
+        for i, s in enumerate(slots):
+            for d in range(nz):
+                at = i * chunk + d * 8
+                part = jnp.concatenate([out_part[at : at + 8], grad_part[at : at + 8]], axis=0)
                 if s:
-                    r["ds"][s, j] = part.astype(BF16)
+                    r["ds"][s, d] = part.astype(BF16)
                 else:
-                    r["down"][j] = part
-        for s in slots:
-            if s:
-                live["dx", BACK[s]] = send(
-                    r["ds"].at[s], r["dr"].at[BACK[s]], "dx", s, BACK[s], at_x(OFFSETS[s])
-                )
+                    r["down"][d] = part
+        for k in (*far_first(nz), 0):
+            part = lax.rem(z + k, nz)
+            for s in slots:
+                if s:
+                    live["dx", BACK[s], k] = send(
+                        r["ds"].at[s, part], r["dr"].at[BACK[s], part], "dx", (s, k), (BACK[s], k), at_x(OFFSETS[s])
+                    )
 
     first_products(0)
     terms_over_y(0)
+    first_products(1)
+    first_products(2)
+    terms_over_y(1)
+    first_products(3)
+    terms_over_y(2)
+    terms_over_y(3)
     activate(0)
-    first_products(1)
+    activate(1)
     forward(0)
-    terms_over_y(1)
+    activate(2)
     second_products(0)
-    first_products(2)
-    activate(1)
-    terms_over_y(2)
+    activate(3)
     forward(1)
-    activate(2)
+    forward(2)
     second_products(1)
-    forward(2)
+    forward(3)
     second_products(2)
+    second_products(3)
 
     tile = min(256, half)
     tokens_all = rows_of("tg", 0, range(NX))
@@ -273,23 +296,23 @@
             r["tok_t"][...], grad_hidden_all[:, h * half : (h + 1) * half]
         ).astype(BF16)
 
-    for s in (1, 2, 3):
-        live["dx", s].wait_recv()
-    sums = []
-    for j in range(2):
-        value = r["down"][j]
+    def sum_over_x(k):
+        part = lax.rem(z + k, nz)
+        value = r["down"][part]
         for s in (1, 2, 3):
-            value = value + r["dr"][s, j].astype(F32)
-        sums.append(value)
-    for d in range(nz):
-        r["zs"][d] = jnp.concatenate([v[d * 8 : d * 8 + 8] for v in sums], axis=0).astype(BF16)
-    dz = [
-        send(r["zs"].at[lax.rem(z + k, nz)], r["zr"].at[nz - k], "dz", k, nz - k, at_z(k)) for k in far_first(nz)
-    ]
-    total = r["zs"][z].astype(F32)
-    for copy in dz:
-        copy.wait_recv()
-    for k in range(1, nz):
+            live["dx", s, k].wait_recv()
+        for s in (1, 2, 3):
+            value = value + r["dr"][s, part].astype(F32)
+        return value
+
+    dz = {}
+    for k in far_first(nz):
+        part = lax.rem(z + k, nz)
+        r["zs"][part] = sum_over_x(k).astype(BF16)
+        dz[k] = send(r["zs"].at[part], r["zr"].at[nz - k], "dz", k, nz - k, at_z(k))
+    total = sum_over_x(0)
+    for k in far_first(nz):
+        dz[nz - k].wait_recv()
         total = total + r["zr"][k].astype(F32)
     out_ref[...] = total[:8].astype(BF16)
     gt_ref[...] = total[8:].astype(BF16)
@@ -301,7 +324,7 @@
     width, hid = w_in.shape
     scratch = scratch_list(ny, nz, width, hid)
     vmem = pl.BlockSpec(memory_space=pltpu.VMEM)
-    any_space = pl.BlockSpec(memory_space=pl.ANY)
+    hbm = pl.BlockSpec(memory_space=pltpu.HBM)
     return pl.pallas_call(
         functools.partial(kernel, ny, nz, tuple(scratch)),
         out_shape=(
@@ -310,11 +333,11 @@
             jax.ShapeDtypeStruct((width, hid), BF16),
             jax.ShapeDtypeStruct((hid, width), BF16),
         ),
-        in_specs=[vmem, vmem, any_space, any_space],
+        in_specs=[vmem, vmem, hbm, hbm],
         out_specs=(vmem, vmem, vmem, vmem),
         scratch_shapes=list(scratch.values()),
         compiler_params=pltpu.CompilerParams(
-            collective_id=0, has_side_effects=True, vmem_limit_bytes=48 * 1024 * 1024
+            collective_id=0, has_side_effects=True, vmem_limit_bytes=51 * 1024 * 1024
         ),
         name="ffn",
     )(tokens, grad_out, w_in, w_out)

time: 77.5 us -> 68.6 us (0.89)
  Pallas kernels: 69.4 us -> 62.6 us
  local copies, waits for them, and re-layouts: 7.17 us -> 4.63 us
    pallas_call x1, Pallas kernels: 69.4 us -> 62.6 us  [local(): pl.pallas_call(functools.partial(kernel, ny, nz, tuple(scratch)), out_sha...]
    unnamed x12 -> x8, local copies, waits for them, and re-layouts: 7.17 us -> 4.63 us
where the time goes in v2:
time: 68.6 us; the launch traced here: 67.9 us
  Pallas kernels  62.6 us (91%)
  local copies, waits for them, and re-layouts  4.63 us (7%)
    pallas_call x1, Pallas kernels, local(): pl.pallas_call(functools.partial(kernel, ny, nz, tuple(scratch)), out_sha...  62.6 us
    unnamed x8, local copies, waits for them, and re-layouts  4.63 us

profile of v2, /device:TPU:1, one launch (start us, length us, event | category | flops | bytes accessed | tf_op | source)
XLA Modules:
  0.0 67.9 jit_solution(11376870942637278888)
XLA Ops:
  0.6 0.0 copy-start
  0.6 0.7 %copy-done = bf16[8,768]{1,0:T(8,128)(2,1)S(1)} copy-done((bf16[8,768]{1,0:T(8,128)(2,1)S(1)}, bf16[8,768]{1,0:T(8,128)(2,1)}, u32[]{:S(2)}) %copy-start) | copy-done | bytes 12312
  1.3 0.0 copy-start.1
  1.3 0.7 %copy-done.1 = bf16[8,768]{1,0:T(8,128)(2,1)S(1)} copy-done((bf16[8,768]{1,0:T(8,128)(2,1)S(1)}, bf16[8,768]{1,0:T(8,128)(2,1)}, u32[]{:S(2)}) %copy-start.1) | copy-done | bytes 12312
  2.0 62.6 %ffn.1 = (bf16[8,768]{1,0:T(8,128)(2,1)S(1)}, bf16[8,768]{1,0:T(8,128)(2,1)S(1)}, bf16[768,768]{1,0:T(8,128)(2,1)S(1)}, bf16[768,768]{1,0:T(8,128)(2,1)S(1)}) custom-call(bf16[8,768]{1,0:T(8,128)(2,1)S(1)} %copy-done, bf16[8,768]{1,0:T(8,128)(2,1)S(1)} %copy-done.1, bf16[768,768]{1,0:T(8,128)(2,1)} %win_hbm.1, bf16[768,768]{1,0:T(8,128)(2,1)} %wout_hbm.1), custom_call_target="tpu_custom_call" | custom-call | tf_op jit(solution)/shard_map/ffn/pallas_call | solution.py:328
  64.6 0.6 copy.12
  65.2 0.6 copy.13
  65.8 1.0 %copy.14 = bf16[768,768]{1,0:T(8,128)(2,1)} copy(bf16[768,768]{1,0:T(8,128)(2,1)S(1)} %get-tuple-element.10) | data formatting | bytes 2359296
  66.8 1.0 %copy.15 = bf16[768,768]{1,0:T(8,128)(2,1)} copy(bf16[768,768]{1,0:T(8,128)(2,1)S(1)} %get-tuple-element.11) | data formatting | bytes 2359296
Async XLA Ops:
  0.6 0.7 %copy-start = (bf16[8,768]{1,0:T(8,128)(2,1)S(1)}, bf16[8,768]{1,0:T(8,128)(2,1)}, u32[]{:S(2)}) copy-start(bf16[8,768]{1,0:T(8,128)(2,1)} %tok_ref.1) | copy-start | bytes 36868
  1.3 0.7 %copy-start.1 = (bf16[8,768]{1,0:T(8,128)(2,1)S(1)}, bf16[8,768]{1,0:T(8,128)(2,1)}, u32[]{:S(2)}) copy-start(bf16[8,768]{1,0:T(8,128)(2,1)} %grad_ref.1) | copy-start | bytes 36868

commit v3 on v2

--- a/solution.py
+++ b/solution.py
@@ -14,9 +14,13 @@
 BF16 = jnp.bfloat16
 
 NX = 4
+NEAR_LAG = 7
 OFFSETS = (0, 1, 3, 2)
 BACK = (0, 2, 1, 3)
 GROUPS = ((0,), (1,), (2,), (3,))
+
+
+SEQUENCE = ((0, 0), (1, 0), (0, 3), (1, 3), (2, 0), (0, 1), (0, 2), (1, 1), (1, 2), (3, 0), (2, 3), (4, 0), (2, 1), (2, 2), (3, 3), (4, 3), (3, 1), (3, 2), (4, 1), (4, 2))
 
 
 def gelu_parts(hidden):
@@ -154,19 +158,24 @@
     az = {k: send(comb.at[0, z], comb.at[0, z], "az", k, nz - k, at_z(k)) for k in near_first(nz)}
     ax = {}
 
-    def block_over_x(k):
+    def block_over_x(k, slots):
         part = lax.rem(z + k, nz)
-        for s in (3, 1, 2):
+        for s in slots:
             ax[BACK[s], k] = send(
                 comb.at[0, part], comb.at[BACK[s], part], "ax", (s, k), (BACK[s], k), at_x(OFFSETS[s])
             )
 
-    block_over_x(0)
+    block_over_x(0, (3, 1, 2))
     for copy in weight_copies:
         copy.wait()
-    for k in near_first(nz):
+    order = near_first(nz)
+    for i, k in enumerate(order):
         az[nz - k].wait_recv()
-        block_over_x(k)
+        block_over_x(k, (3,))
+        if i >= NEAR_LAG:
+            block_over_x(order[i - NEAR_LAG], (1, 2))
+    for k in order[len(order) - NEAR_LAG :]:
+        block_over_x(k, (1, 2))
 
     def split_chunk(s):
         block = comb[s].astype(F32)
@@ -260,26 +269,8 @@
                         r["ds"].at[s, part], r["dr"].at[BACK[s], part], "dx", (s, k), (BACK[s], k), at_x(OFFSETS[s])
                     )
 
-    first_products(0)
-    terms_over_y(0)
-    first_products(1)
-    first_products(2)
-    terms_over_y(1)
-    first_products(3)
-    terms_over_y(2)
-    terms_over_y(3)
-    activate(0)
-    activate(1)
-    forward(0)
-    activate(2)
-    second_products(0)
-    activate(3)
-    forward(1)
-    forward(2)
-    second_products(1)
-    forward(3)
-    second_products(2)
-    second_products(3)
+    for step, g in SEQUENCE:
+        (first_products, terms_over_y, activate, forward, second_products)[step](g)
 
     tile = min(256, half)
     tokens_all = rows_of("tg", 0, range(NX))
@@ -325,7 +316,7 @@
     scratch = scratch_list(ny, nz, width, hid)
     vmem = pl.BlockSpec(memory_space=pltpu.VMEM)
     hbm = pl.BlockSpec(memory_space=pltpu.HBM)
-    return pl.pallas_call(
+    results = pl.pallas_call(
         functools.partial(kernel, ny, nz, tuple(scratch)),
         out_shape=(
             jax.ShapeDtypeStruct((8, width), BF16),
@@ -341,6 +332,25 @@
         ),
         name="ffn",
     )(tokens, grad_out, w_in, w_out)
+    anywhere = pl.BlockSpec(memory_space=pl.ANY)
+    return pl.pallas_call(
+        write_out,
+        out_shape=tuple(jax.ShapeDtypeStruct(a.shape, a.dtype) for a in results),
+        in_specs=[anywhere] * 4,
+        out_specs=(anywhere,) * 4,
+        scratch_shapes=[pltpu.SemaphoreType.DMA((4,))],
+        compiler_params=pltpu.CompilerParams(vmem_limit_bytes=1024 * 1024),
+        name="write_out",
+    )(*results)
+
+
+def write_out(*refs):
+    sources, targets, sem = refs[:4], refs[4:8], refs[8]
+    copies = [pltpu.make_async_copy(a, b, sem.at[i]) for i, (a, b) in enumerate(zip(sources, targets))]
+    for copy in copies[::-1]:
+        copy.start()
+    for copy in copies:
+        copy.wait()
 
 
 def solution(mesh):

time: 68.6 us -> 63.6 us (0.927)
  local copies, waits for them, and re-layouts: 4.63 us -> 1.41 us
  Pallas kernels: 62.6 us -> 61.3 us
    unnamed x8 -> x4, local copies, waits for them, and re-layouts: 4.63 us -> 1.41 us
    pallas_call x1, Pallas kernels: 62.6 us -> 59.9 us  [local(): pl.pallas_call(functools.partial(kernel, ny, nz, tuple(scratch)), out_sha...]
    pallas_call x0 -> x1, Pallas kernels: none -> 1.44 us  [local(): pl.pallas_call(write_out, out_shape=tuple((jax.ShapeDtypeStruct(a.shape,...]
where the time goes in v3:
time: 63.6 us; the launch traced here: 63.4 us
  Pallas kernels  61.3 us (96%)
  local copies, waits for them, and re-layouts  1.41 us (2%)
  between operations  0.65 us (1%)
    pallas_call x1, Pallas kernels, local(): pl.pallas_call(functools.partial(kernel, ny, nz, tuple(scratch)), out_sha...  59.9 us
    pallas_call x1, Pallas kernels, local(): pl.pallas_call(write_out, out_shape=tuple((jax.ShapeDtypeStruct(a.shape,...  1.44 us
    unnamed x4, local copies, waits for them, and re-layouts  1.41 us

profile of v3, /device:TPU:1, one launch (start us, length us, event | category | flops | bytes accessed | tf_op | source)
XLA Modules:
  0.0 63.4 jit_solution(2075139916886906001)
XLA Ops:
  0.6 0.0 copy-start
  0.6 0.7 %copy-done = bf16[8,768]{1,0:T(8,128)(2,1)S(1)} copy-done((bf16[8,768]{1,0:T(8,128)(2,1)S(1)}, bf16[8,768]{1,0:T(8,128)(2,1)}, u32[]{:S(2)}) %copy-start) | copy-done | bytes 12312
  1.3 0.0 copy-start.1
  1.3 0.7 %copy-done.1 = bf16[8,768]{1,0:T(8,128)(2,1)S(1)} copy-done((bf16[8,768]{1,0:T(8,128)(2,1)S(1)}, bf16[8,768]{1,0:T(8,128)(2,1)}, u32[]{:S(2)}) %copy-start.1) | copy-done | bytes 12312
  2.0 59.9 %ffn.1 = (bf16[8,768]{1,0:T(8,128)(2,1)S(1)}, bf16[8,768]{1,0:T(8,128)(2,1)S(1)}, bf16[768,768]{1,0:T(8,128)(2,1)S(1)}, bf16[768,768]{1,0:T(8,128)(2,1)S(1)}) custom-call(bf16[8,768]{1,0:T(8,128)(2,1)S(1)} %copy-done, bf16[8,768]{1,0:T(8,128)(2,1)S(1)} %copy-done.1, bf16[768,768]{1,0:T(8,128)(2,1)} %win_hbm.1, bf16[768,768]{1,0:T(8,128)(2,1)} %wout_hbm.1), custom_call_target="tpu_custom_call" | custom-call | tf_op jit(solution)/shard_map/ffn/pallas_call | solution.py:319
  61.9 1.4 %write_out.1 = (bf16[8,768]{1,0:T(8,128)(2,1)}, bf16[8,768]{1,0:T(8,128)(2,1)}, bf16[768,768]{1,0:T(8,128)(2,1)}, bf16[768,768]{1,0:T(8,128)(2,1)}) custom-call(bf16[8,768]{1,0:T(8,128)(2,1)S(1)} %get-tuple-element.8.refs_0_, bf16[8,768]{1,0:T(8,128)(2,1)S(1)} %get-tuple-element.9.refs_1_, bf16[768,768]{1,0:T(8,128)(2,1)S(1)} %get-tuple-element.10.refs_2_, ...), custom_call_target="tpu_custom_call" | custom-call | tf_op jit(solution)/shard_map/write_out/pallas_call | solution.py:336
Async XLA Ops:
  0.6 0.7 %copy-start = (bf16[8,768]{1,0:T(8,128)(2,1)S(1)}, bf16[8,768]{1,0:T(8,128)(2,1)}, u32[]{:S(2)}) copy-start(bf16[8,768]{1,0:T(8,128)(2,1)} %tok_ref.1) | copy-start | bytes 36868
  1.3 0.7 %copy-start.1 = (bf16[8,768]{1,0:T(8,128)(2,1)S(1)}, bf16[8,768]{1,0:T(8,128)(2,1)}, u32[]{:S(2)}) copy-start(bf16[8,768]{1,0:T(8,128)(2,1)} %grad_ref.1) | copy-start | bytes 36868

commit v4 on v3

--- a/solution.py
+++ b/solution.py
@@ -166,8 +166,6 @@
             )
 
     block_over_x(0, (3, 1, 2))
-    for copy in weight_copies:
-        copy.wait()
     order = near_first(nz)
     for i, k in enumerate(order):
         az[nz - k].wait_recv()
@@ -176,6 +174,8 @@
             block_over_x(order[i - NEAR_LAG], (1, 2))
     for k in order[len(order) - NEAR_LAG :]:
         block_over_x(k, (1, 2))
+    for copy in weight_copies:
+        copy.wait()
 
     def split_chunk(s):
         block = comb[s].astype(F32)

time: 63.6 us -> 63.6 us (level)
  no operation moved by 1% of the time
where the time goes in v4:
time: 63.6 us; the launch traced here: 63.4 us
  Pallas kernels  61.3 us (96%)
  local copies, waits for them, and re-layouts  1.41 us (2%)
  between operations  0.65 us (1%)
    pallas_call x1, Pallas kernels, local(): pl.pallas_call(functools.partial(kernel, ny, nz, tuple(scratch)), out_sha...  59.9 us
    pallas_call x1, Pallas kernels, local(): pl.pallas_call(write_out, out_shape=tuple((jax.ShapeDtypeStruct(a.shape,...  1.44 us
    unnamed x4, local copies, waits for them, and re-layouts  1.41 us

profile of v4, /device:TPU:1, one launch (start us, length us, event | category | flops | bytes accessed | tf_op | source)
XLA Modules:
  0.0 63.4 jit_solution(2758121803646416060)
XLA Ops:
  0.6 0.0 copy-start
  0.6 0.7 %copy-done = bf16[8,768]{1,0:T(8,128)(2,1)S(1)} copy-done((bf16[8,768]{1,0:T(8,128)(2,1)S(1)}, bf16[8,768]{1,0:T(8,128)(2,1)}, u32[]{:S(2)}) %copy-start) | copy-done | bytes 12312
  1.3 0.0 copy-start.1
  1.3 0.7 %copy-done.1 = bf16[8,768]{1,0:T(8,128)(2,1)S(1)} copy-done((bf16[8,768]{1,0:T(8,128)(2,1)S(1)}, bf16[8,768]{1,0:T(8,128)(2,1)}, u32[]{:S(2)}) %copy-start.1) | copy-done | bytes 12312
  2.0 59.9 %ffn.1 = (bf16[8,768]{1,0:T(8,128)(2,1)S(1)}, bf16[8,768]{1,0:T(8,128)(2,1)S(1)}, bf16[768,768]{1,0:T(8,128)(2,1)S(1)}, bf16[768,768]{1,0:T(8,128)(2,1)S(1)}) custom-call(bf16[8,768]{1,0:T(8,128)(2,1)S(1)} %copy-done, bf16[8,768]{1,0:T(8,128)(2,1)S(1)} %copy-done.1, bf16[768,768]{1,0:T(8,128)(2,1)} %win_hbm.1, bf16[768,768]{1,0:T(8,128)(2,1)} %wout_hbm.1), custom_call_target="tpu_custom_call" | custom-call | tf_op jit(solution)/shard_map/ffn/pallas_call | solution.py:319
  61.9 1.4 %write_out.1 = (bf16[8,768]{1,0:T(8,128)(2,1)}, bf16[8,768]{1,0:T(8,128)(2,1)}, bf16[768,768]{1,0:T(8,128)(2,1)}, bf16[768,768]{1,0:T(8,128)(2,1)}) custom-call(bf16[8,768]{1,0:T(8,128)(2,1)S(1)} %get-tuple-element.8.refs_0_, bf16[8,768]{1,0:T(8,128)(2,1)S(1)} %get-tuple-element.9.refs_1_, bf16[768,768]{1,0:T(8,128)(2,1)S(1)} %get-tuple-element.10.refs_2_, ...), custom_call_target="tpu_custom_call" | custom-call | tf_op jit(solution)/shard_map/write_out/pallas_call | solution.py:336
Async XLA Ops:
  0.6 0.7 %copy-start = (bf16[8,768]{1,0:T(8,128)(2,1)S(1)}, bf16[8,768]{1,0:T(8,128)(2,1)}, u32[]{:S(2)}) copy-start(bf16[8,768]{1,0:T(8,128)(2,1)} %tok_ref.1) | copy-start | bytes 36868
  1.3 0.7 %copy-start.1 = (bf16[8,768]{1,0:T(8,128)(2,1)S(1)}, bf16[8,768]{1,0:T(8,128)(2,1)}, u32[]{:S(2)}) copy-start(bf16[8,768]{1,0:T(8,128)(2,1)} %grad_ref.1) | copy-start | bytes 36868
